TPU v7x, 512 devices: a whole 4x8x8 slice. The times are simulated.
512 devices in a mesh: dp: 8 (over x, core), proto: 64 (over z, y).
Axes of the slice: x: 4, y: 8, z: 8, core: 2. Of those that a mesh axis runs over, the one named last changes fastest.
Arguments:
- embeddings: bfloat16 [1024, 512], P('dp'), may hold values from -0.25 to 0.25
- prototypes: bfloat16 [131072, 512], P('proto'), may hold values from -0.25 to 0.25
- embedding_log_potential: float32 [1024], P('dp'), may hold values from -1.5 to 1.5
- prototype_log_potential: float32 [131072], P('proto'), may hold values from -1.5 to 1.5
- scaled_plan_gradient: bfloat16 [1024, 131072], P('dp', 'proto'), may hold values from -14 to 14
Outputs:
- grad_emb: float32 [1024, 512], P('dp', 'proto')
- grad_proto: bfloat16 [131072, 512], P('proto', 'dp')
All inputs are finite; a program needn't handle non-finite values.
Results may differ from a plain program's by a relative error of at most 0.03.
Values may be sent and summed in bfloat16 or wider, within the bound.
A program may use at most 64 MiB of HBM per device.

v0:
```python
import math

import jax
import jax.numpy as jnp
from jax import lax
from jax.sharding import PartitionSpec as P

ITERS = 3


ENTROPY_TEMP_SCALE = 0.05
RIDGE_TERM = 0.05
HIGHEST_PREC = lax.Precision.HIGHEST


def combine(former, factor, latter):
    return (former[0] + factor * latter[0], former[1] + factor * latter[1])


def shards(
    embeddings, prototypes, embedding_log_potential, prototype_log_potential, scaled_plan_gradient
):
    n_dp = lax.axis_size("dp")
    n_proto = lax.axis_size("proto")
    n_total = embeddings.shape[0] * n_dp
    k_total = prototypes.shape[0] * n_proto
    root_rows = math.sqrt(n_total)
    root_cols = math.sqrt(k_total)
    similarity_scores = lax.dot_general(
        embeddings, prototypes, (((1,), (1,)), ((), ())), preferred_element_type=jnp.float32
    )
    gibbs_kernel_matrix = jnp.exp(
        similarity_scores / ENTROPY_TEMP_SCALE
        + embedding_log_potential[:, None]
        + prototype_log_potential[None, :]
    )
    weighted = scaled_plan_gradient.astype(jnp.float32) * gibbs_kernel_matrix
    row_sums, rhs_rows = lax.psum(
        (jnp.sum(gibbs_kernel_matrix, axis=1), jnp.sum(weighted, axis=1)), "proto"
    )
    col_sums, rhs_cols = lax.psum(
        (jnp.sum(gibbs_kernel_matrix, axis=0), jnp.sum(weighted, axis=0)), "dp"
    )
    row_marg = row_sums / k_total + RIDGE_TERM
    col_marg = col_sums / n_total + RIDGE_TERM
    rhs = (rhs_rows / root_cols, rhs_cols / root_rows)
    coupling = 1.0 / (root_rows * root_cols)

    def local_inner(former, latter):
        return jnp.sum(former[0] * latter[0]) / n_proto + jnp.sum(former[1] * latter[1]) / n_dp

    solution = (jnp.zeros_like(rhs[0]), jnp.zeros_like(rhs[1]))
    residual = rhs

    def global_norm(vector):
        return lax.psum(local_inner(vector, vector), ("dp", "proto"))

    direction = rhs
    res_norm = global_norm(residual)
    for iteration in range(ITERS):
        row_part = lax.psum(
            jnp.dot(gibbs_kernel_matrix, direction[1], precision=HIGHEST_PREC), "proto"
        )
        col_part = lax.psum(
            jnp.dot(direction[0], gibbs_kernel_matrix, precision=HIGHEST_PREC), "dp"
        )
        image = (
            row_marg * direction[0] + coupling * row_part,
            col_marg * direction[1] + coupling * col_part,
        )
        step_size = res_norm / lax.psum(local_inner(direction, image), ("dp", "proto"))
        solution = combine(solution, step_size, direction)
        residual = combine(residual, -step_size, image)
        new_norm = global_norm(residual)
        direction = combine(residual, new_norm / res_norm, direction)
        res_norm = new_norm
    implicit_adjustment = solution[0][:, None] / root_cols + solution[1][None, :] / root_rows
    prototype_weight = (
        gibbs_kernel_matrix
        * (scaled_plan_gradient.astype(jnp.float32) - implicit_adjustment)
        / ENTROPY_TEMP_SCALE
    ).astype(jnp.bfloat16)
    emb_terms = jnp.dot(prototype_weight, prototypes, preferred_element_type=jnp.float32)
    grad_emb = lax.psum_scatter(emb_terms, "proto", scatter_dimension=1, tiled=True)
    proto_terms = lax.dot_general(
        prototype_weight, embeddings, (((0,), (0,)), ((), ())), preferred_element_type=jnp.float32
    )
    grad_proto = lax.psum_scatter(
        proto_terms.astype(jnp.bfloat16), "dp", scatter_dimension=1, tiled=True
    )
    return (grad_emb, grad_proto)


def solution(mesh):
    return jax.shard_map(
        shards,
        mesh=mesh,
        in_specs=(P("dp", None), P("proto", None), P("dp"), P("proto"), P("dp", "proto")),
        out_specs=(P("dp", "proto"), P("proto", "dp")),
        check_vma=False,
    )
```

profile of v0, /device:TPU:1, one launch (start us, length us, event | category | flops | bytes accessed | tf_op | source)
XLA Modules:
  0.0 1154.7 jit_solution(4264202572133326285)
XLA Ops:
  8.1 1.5 copy-done
  9.6 2.0 fusion.6
  11.6 18.9 %psum.113 = f32[2048]{0:T(1024)S(1)} all-reduce(f32[2048]{0:T(1024)S(1)} %get-tuple-element.2), channel_id=1, replica_groups=mesh['dp'=8,'proto'=64] {'dp'}, use_global_device_ids=true, to_apply=%region_4.0 | all-reduce | flops 2048 | bytes 16384 | tf_op jit(solution)/shard_map/psum | solution.py:41
  30.5 0.9 convolution_bitcast_fusion.2
  31.4 116.6 %all-reduce.2 = (f32[128]{0:T(128)S(1)}, f32[128]{0:T(128)S(1)}, f32[128]{0:T(128)S(1)}) all-reduce(f32[128]{0:T(128)S(1)} %get-tuple-element.3, f32[128]{0:T(128)S(1)} %convolution_bitcast_fusion.2, f32[128]{0:T(128)S(1)} %get-tuple-element.4), channel_id=1, replica_groups=mesh['dp'=8,'proto'=64] {'proto'}, use_global_device_ids=true, to_apply=%region_1.0 | all-reduce | flops 384 | bytes 3072 | tf_op jit(solution)/shard_map/psum | solution.py:38
  150.5 50.8 %all-reduce.3 = (f32[2048]{0:T(1024)S(1)}, f32[2048]{0:T(1024)S(1)}) all-reduce(f32[2048]{0:T(1024)S(1)} %bitcast.39, f32[2048]{0:T(1024)S(1)} %get-tuple-element.5), channel_id=1, replica_groups=mesh['dp'=8,'proto'=64] {'dp'}, use_global_device_ids=true, to_apply=%region_13.0 | all-reduce | flops 4096 | bytes 32768 | tf_op jit(solution)/shard_map/psum | solution.py:64
  203.3 95.1 %all-reduce.1 = (f32[]{:T(128)}, f32[]{:T(128)}) all-reduce(f32[]{:T(128)S(6)} %add.153, f32[]{:T(128)S(6)} %add.160), channel_id=1, replica_groups=mesh['dp'=8,'proto'=64] {'dp','proto'}, use_global_device_ids=true, to_apply=%region_6.0 | all-reduce | flops 2 | bytes 16 | tf_op jit(solution)/shard_map/psum | solution.py:56
  302.4 95.5 %psum.120 = f32[]{:T(128)} all-reduce(f32[]{:T(128)S(6)} %add.163), channel_id=1, replica_groups=mesh['dp'=8,'proto'=64] {'dp','proto'}, use_global_device_ids=true, to_apply=%region_18.0 | all-reduce | flops 1 | bytes 8 | tf_op jit(solution)/shard_map/psum | solution.py:56
  399.8 12.6 %psum.122 = f32[2048]{0:T(1024)S(1)} all-reduce(f32[2048]{0:T(1024)S(1)} %bitcast.41), channel_id=1, replica_groups=mesh['dp'=8,'proto'=64] {'dp'}, use_global_device_ids=true, to_apply=%region_21.0 | all-reduce | flops 2048 | bytes 16384 | tf_op jit(solution)/shard_map/psum | solution.py:64
  413.7 0.9 convolution_bitcast_fusion.1
  414.6 112.0 %psum.121 = f32[128]{0:T(128)S(1)} all-reduce(f32[128]{0:T(128)S(1)} %convolution_bitcast_fusion.1), channel_id=1, replica_groups=mesh['dp'=8,'proto'=64] {'proto'}, use_global_device_ids=true, to_apply=%region_19.0 | all-reduce | flops 128 | bytes 1024 | tf_op jit(solution)/shard_map/psum | solution.py:61
  527.9 120.9 %psum.123 = f32[]{:T(128)} all-reduce(f32[]{:T(128)S(6)} %add.168), channel_id=1, replica_groups=mesh['dp'=8,'proto'=64] {'dp','proto'}, use_global_device_ids=true, to_apply=%region_23.0 | all-reduce | flops 1 | bytes 8 | tf_op jit(solution)/shard_map/psum | solution.py:71
  652.8 95.5 %psum.124 = f32[]{:T(128)} all-reduce(f32[]{:T(128)S(6)} %add.172), channel_id=1, replica_groups=mesh['dp'=8,'proto'=64] {'dp','proto'}, use_global_device_ids=true, to_apply=%region_26.0 | all-reduce | flops 1 | bytes 8 | tf_op jit(solution)/shard_map/psum | solution.py:56
  750.3 12.6 %psum.126 = f32[2048]{0:T(1024)S(1)} all-reduce(f32[2048]{0:T(1024)S(1)} %bitcast.42), channel_id=1, replica_groups=mesh['dp'=8,'proto'=64] {'dp'}, use_global_device_ids=true, to_apply=%region_29.0 | all-reduce | flops 2048 | bytes 16384 | tf_op jit(solution)/shard_map/psum | solution.py:64
  764.2 0.9 convolution_bitcast_fusion
  765.1 112.1 %psum.125 = f32[128]{0:T(128)S(1)} all-reduce(f32[128]{0:T(128)S(1)} %convolution_bitcast_fusion), channel_id=1, replica_groups=mesh['dp'=8,'proto'=64] {'proto'}, use_global_device_ids=true, to_apply=%region_27.0 | all-reduce | flops 128 | bytes 1024 | tf_op jit(solution)/shard_map/psum | solution.py:61
  878.4 120.9 %psum.127 = f32[]{:T(128)} all-reduce(f32[]{:T(128)S(6)} %add.177), channel_id=1, replica_groups=mesh['dp'=8,'proto'=64] {'dp','proto'}, use_global_device_ids=true, to_apply=%region_31.0 | all-reduce | flops 1 | bytes 8 | tf_op jit(solution)/shard_map/psum | solution.py:71
  1000.7 1.3 fusion.5
  1002.1 0.8 copy-done.1
  1002.8 1.7 fusion.14
  1004.6 3.1 convolution_convert_fusion
  1007.8 1.3 dynamic-slice
  1009.7 136.2 %all-reduce.6.cloned.1.call-done = f32[128,512]{0,1:T(8,128)} async-done(((f32[128,512]{0,1:T(8,128)}), f32[128,512]{0,1:T(8,128)}) %all-reduce.6.cloned.1.call-update) | async-done | bytes 262160
  1145.9 1.3 constant_dynamic-slice_fusion
  (27 shorter events, 8.2 us)
Async XLA Ops:
  8.0 1.6 copy-start
  8.0 1137.9 %all-reduce.6.cloned.1.call-start = ((), (), s32[]{:S(2)}) async-start(), calls=%async_computation.2 | async-start | bytes 524288
  1002.0 0.8 copy-start.1
  1002.8 1.7 copy-start.2
  1004.5 142.7 %reduce-scatter.2.cloned.1.call-start = ((), (), s32[]{:S(2)}) async-start(), calls=%async_computation.1 | async-start | bytes 2359296 | tf_op jit(solution)/shard_map/reduce_scatter | solution.py:88
Sparse Core Ops, SparseCore 0:
  1004.7 141.2 all-reduce.5
Sparse Core Ops, SparseCore 1:
  1008.7 30.5 reduce-scatter.1
where the time goes:
time: 1160 us; the launch traced here: 1150 us
  blocking collectives  964 us (83%)
  waiting for transfers between devices  136 us (12%)
  between operations  30.8 us (3%)
    psum x3, blocking collectives, global_norm(): return lax.psum(local_inner(vector, vector), ('dp', 'proto'))  286 us
    psum x2, blocking collectives, shards(): lax.psum(local_inner(direction, image), ('dp', 'proto'))  242 us
    psum x2, blocking collectives, shards(): lax.psum(jnp.dot(gibbs_kernel_matrix, direction[1], precision=HIGHEST_PRE...  224 us
    unnamed x3, waiting for transfers between devices  136 us
    psum x1, blocking collectives, shards(): lax.psum((jnp.sum(gibbs_kernel_matrix, axis=1), jnp.sum(weighted, axis=1)...  117 us
    psum x3, blocking collectives, shards(): lax.psum(jnp.dot(direction[0], gibbs_kernel_matrix, precision=HIGHEST_PRE...  76.1 us
  transfers between devices with their start and end apart: 2, of which 1 were waited for; matrix products, arithmetic and copies ran while one was open for 0% of the time, Pallas kernels for 0%

commit v1 on v0

v1 whole, which is shorter than its diff:
```python
import functools
import math

import jax
import jax.numpy as jnp
from jax import lax
from jax.experimental import pallas as pl
from jax.experimental.pallas import tpu as pltpu
from jax.sharding import PartitionSpec as P

MESH = pl.DeviceIdType.MESH
TEMP = 0.05
RIDGE = 0.05
N_DP = 8
N_Z = 8
N_Y = 8
N_PROTO = N_Z * N_Y
LANES = 128
F32 = jnp.float32
BF16 = jnp.bfloat16


def total(values):
    return jnp.sum(values, axis=1, keepdims=True)


def as_column(row):
    return jnp.broadcast_to(row, (LANES, LANES)).T


def as_row(acc):
    return jnp.sum(acc.T, axis=0, keepdims=True)


def far_first(i):
    return 4 + (1 - 2 * lax.rem(i, 2)) * lax.div(i + 1, 2)


def wait_bytes(ref, sem):
    pltpu.make_async_copy(ref, ref, sem).wait()


def solve(m0, b1, b2, r1r1, r1w, ww, waw):
    g00, g01, g02 = m0, b1 - r1r1, b2 - r1w
    g11, g12, g22 = r1w + r1r1, ww + r1w, waw
    l10, l20 = g01 / g00, g02 / g00
    d1 = g11 - g01 * l10
    i1 = jnp.where(d1 > 1e-6 * g11, 1.0 / d1, 0.0)
    t = g12 - l20 * g01
    l21 = t * i1
    d2 = g22 - l20 * g02 - l21 * t
    i2 = jnp.where(d2 > 1e-6 * g22, 1.0 / d2, 0.0)
    z1 = b1 - l10 * m0
    z2 = b2 - l20 * m0 - l21 * z1
    y2 = z2 * i2
    y1 = z1 * i1 - l21 * y2
    y0 = 1.0 - l10 * y1 - l20 * y2
    return y0, y1, y2


def body(
    rows_all, cols_all,
    e_hbm, p_hbm, er_hbm, pc_hbm, g_hbm, o_emb, o_proto,
    ev, et, pv, er, pc, gv, kv, wv, td1, td2, td3, tp1, tp2, rs_out, rs_in, gp_out, gp_in,
    in_sem, ready, send, recv,
):
    dp, pr = lax.axis_index("dp"), lax.axis_index("proto")
    z, y = lax.div(pr, N_Y), lax.rem(pr, N_Y)
    cols = pv.shape[0]
    tiles = cols // LANES
    root_cols = math.sqrt(cols_all)
    root_rows = math.sqrt(rows_all)
    coupling = 1.0 / (root_rows * root_cols)

    loads = [
        pltpu.make_async_copy(src, dst, in_sem.at[i])
        for i, (src, dst) in enumerate(
            [(e_hbm, ev), (p_hbm, pv), (er_hbm, er), (pc_hbm, pc), (g_hbm, gv)]
        )
    ]
    for load in loads:
        load.start()

    barrier = pltpu.get_barrier_semaphore()
    for k in range(1, 8):
        pl.semaphore_signal(
            barrier, inc=1, device_id=(lax.rem(dp + k, N_DP), pr), device_id_type=MESH
        )
        pl.semaphore_signal(
            barrier, inc=1, device_id=(dp, z * N_Y + lax.rem(y + k, N_Y)), device_id_type=MESH
        )
        pl.semaphore_signal(
            barrier, inc=1, device_id=(dp, lax.rem(z + k, N_Z) * N_Y + y), device_id_type=MESH
        )
    for load in loads:
        load.wait()

    def to_dp(buf, i):
        for k in range(1, N_DP):
            pltpu.make_async_remote_copy(
                src_ref=buf.at[dp], dst_ref=buf.at[dp], send_sem=send.at[i], recv_sem=recv.at[i],
                device_id=(lax.rem(dp + k, N_DP), pr), device_id_type=MESH,
            ).start()

    def to_proto(make, i):
        @pl.loop(0, N_PROTO - 1)
        def _(t):
            dz, dy = far_first(lax.div(t, N_Y)), far_first(lax.rem(t, N_Y))
            other = lax.rem(z + dz, N_Z) * N_Y + lax.rem(y + dy, N_Y)
            src, dst = make(other)
            pltpu.make_async_remote_copy(
                src_ref=src, dst_ref=dst, send_sem=send.at[i], recv_sem=recv.at[i],
                device_id=(dp, other), device_id_type=MESH,
            ).start()

    er_col = as_column(er[...])
    row_acc = jnp.zeros((LANES, LANES), F32)
    rhs_acc = jnp.zeros((LANES, LANES), F32)
    wide = 256
    er_wide = jnp.concatenate([er_col, er_col], axis=1)
    for c in range(cols // wide):
        at = pl.ds(c * wide, wide)
        scores = lax.dot_general(
            ev[...], pv[at, :], (((1,), (1,)), ((), ())), preferred_element_type=F32
        )
        k = jnp.exp(scores * (1.0 / TEMP) + er_wide + pc[:, at])
        kv[:, at] = k
        w = gv[:, at].astype(F32) * k
        td1[dp, 0:1, at] = jnp.sum(k, axis=0, keepdims=True)
        td1[dp, 1:2, at] = jnp.sum(w, axis=0, keepdims=True)
        row_acc += k[:, :LANES] + k[:, LANES:]
        rhs_acc += w[:, :LANES] + w[:, LANES:]

    pl.semaphore_wait(barrier, 21)
    to_dp(td1, 0)
    for k in range(1, 8):
        pl.semaphore_signal(
            ready, inc=1, device_id=(dp, lax.rem(z + k, N_Z) * N_Y + y), device_id_type=MESH
        )
    row_part = as_row(row_acc)
    rhs_part = as_row(rhs_acc)
    et[...] = jnp.concatenate(
        [ev[:, j * LANES : (j + 1) * LANES].astype(F32).T for j in range(et.shape[0] // LANES)],
        axis=0,
    ).astype(BF16)
    wait_bytes(td1.at[pl.ds(0, N_DP - 1)], recv.at[0])
    col_pair = jnp.sum(td1[...], axis=0)
    dc = col_pair[0:1] * (1.0 / rows_all) + RIDGE
    v0c = col_pair[1:2] * (1.0 / root_rows)

    def lanes(row, t):
        return row[:, t * LANES : (t + 1) * LANES]

    def fold(row):
        return functools.reduce(lambda a, b: a + b, [lanes(row, t) for t in range(tiles)])

    def k_times(*vectors):
        accs = [jnp.zeros((LANES, LANES), F32) for _ in vectors]
        for t in range(tiles):
            k = kv[:, t * LANES : (t + 1) * LANES]
            accs = [a + k * lanes(v, t) for a, v in zip(accs, vectors)]
        return [as_row(a) for a in accs]

    (kv0,) = k_times(v0c)
    tp1[pr] = jnp.concatenate(
        [row_part, rhs_part, kv0, fold(v0c * v0c), fold(v0c * dc * v0c), jnp.zeros((3, LANES), F32)],
        axis=0,
    )
    pl.semaphore_wait(ready, 7)
    to_proto(lambda other: (tp1.at[pr], tp1.at[pr]), 1)
    wait_bytes(tp1.at[pl.ds(0, N_PROTO - 1)], recv.at[1])
    one = jnp.sum(tp1[...], axis=0)
    dr = one[0:1] * (1.0 / cols_all) + RIDGE
    v0r = one[1:2] * (1.0 / root_cols)
    kv0 = one[2:3]
    s0, s1 = total(one[3:4]), total(one[4:5])
    p_r = dr * v0r + coupling * kv0

    v0_col, p_col = as_column(v0r), as_column(p_r)
    for t in range(tiles):
        at = pl.ds(t * LANES, LANES)
        k = kv[:, at]
        td2[dp, 0:1, at] = jnp.sum(k * v0_col, axis=0, keepdims=True)
        td2[dp, 1:2, at] = jnp.sum(k * p_col, axis=0, keepdims=True)
    td2[dp, 0:1, pl.ds(cols, LANES)] = v0r * v0r
    td2[dp, 1:2, pl.ds(cols, LANES)] = v0r * (dr * v0r + (2.0 * coupling) * kv0)
    to_dp(td2, 2)
    wait_bytes(td2.at[pl.ds(0, N_DP - 1)], recv.at[2])
    two = jnp.sum(td2[...], axis=0)
    m0 = s0 + total(two[0:1, cols:])
    m1 = s1 + total(two[1:2, cols:])
    theta = m1 / m0
    step = m0 / m1
    ktv0, ktp = two[0:1, :cols], two[1:2, :cols]
    r1r = v0r - step * p_r
    r1c = v0c - step * (dc * v0c + coupling * ktv0)
    ktr1 = ktv0 - step * ktp
    wc = step * (dc * r1c + coupling * ktr1) - r1c

    kr1, kw = k_times(r1c, wc)
    tp2[pr] = jnp.concatenate(
        [kr1, kw, fold(r1c * r1c), fold(r1c * wc), fold(v0c * wc), fold(wc * wc),
         fold(wc * dc * wc), fold(v0c * r1c)],
        axis=0,
    )
    to_proto(lambda other: (tp2.at[pr], tp2.at[pr]), 3)
    wait_bytes(tp2.at[pl.ds(0, N_PROTO - 1)], recv.at[3])
    three = jnp.sum(tp2[...], axis=0)
    kr1, kw = three[0:1], three[1:2]
    wr = step * (dr * r1r + coupling * kr1) - r1r
    td3[dp] = jnp.concatenate(
        [r1r * r1r, r1r * wr, v0r * wr, wr * wr, wr * (dr * wr + (2.0 * coupling) * kw), v0r * r1r,
         jnp.zeros((2, LANES), F32)],
        axis=0,
    )
    to_dp(td3, 4)
    wait_bytes(td3.at[pl.ds(0, N_DP - 1)], recv.at[4])
    four = total(jnp.sum(td3[...], axis=0))
    five = total(three)
    r1r1, r1w = four[0:1] + five[2:3], four[1:2] + five[3:4]
    v0w, ww = four[2:3] + five[4:5], four[3:4] + five[5:6]
    waw = (four[4:5] + five[6:7]) * step
    v0r1 = four[5:6] + five[7:8]
    y0, y1, y2 = solve(m0, v0r1, v0w, r1r1, r1w, ww, waw)
    y0, y1, y2 = y0 * step, y1 * step, y2 * step
    sol_r = (y0 * v0r + y1 * r1r + y2 * wr) * (1.0 / root_cols)
    sol_c = (y0 * v0c + y1 * r1c + y2 * wc) * (1.0 / root_rows)

    sol_col = as_column(sol_r)
    for t in range(tiles):
        at = pl.ds(t * LANES, LANES)
        g = gv[:, at].astype(F32)
        wv[:, at] = (kv[:, at] * (g - sol_col - lanes(sol_c, t)) * (1.0 / TEMP)).astype(BF16)
    ge = jnp.dot(wv[...], pv[...], preferred_element_type=F32)
    for j in range(4):
        rs_out[pl.ds(16 * j, 16)] = ge[:, j * LANES : (j + 1) * LANES].T.reshape(16, 8, LANES)
    to_proto(lambda other: (rs_out.at[other], rs_in.at[pr]), 5)
    rs_in[pr] = rs_out[pr]

    def proto_terms(d):
        part = et[pl.ds(pl.multiple_of(d * 64, 64), 64), :]
        gp_out[d] = jnp.dot(part, wv[...], preferred_element_type=F32).astype(BF16)

    for k in range(1, N_DP):
        d = lax.rem(dp + k, N_DP)
        proto_terms(d)
        pltpu.make_async_remote_copy(
            src_ref=gp_out.at[d], dst_ref=gp_in.at[dp], send_sem=send.at[6], recv_sem=recv.at[6],
            device_id=(d, pr), device_id_type=MESH,
        ).start()
    proto_terms(dp)
    gp_in[dp] = gp_out[dp]
    wait_bytes(rs_in.at[pl.ds(0, N_PROTO - 1)], recv.at[5])
    o_emb[...] = jnp.sum(rs_in[...], axis=0)
    wait_bytes(gp_in.at[pl.ds(0, N_DP - 1)], recv.at[6])
    for c in range(cols // 512):
        at = pl.ds(c * 512, 512)
        acc = gp_in[0, :, at].astype(F32)
        for d in range(1, N_DP):
            acc += gp_in[d, :, at].astype(F32)
        o_proto[:, at] = acc.astype(BF16)

    wait_bytes(td1.at[pl.ds(0, N_DP - 1)], send.at[0])
    wait_bytes(tp1.at[pl.ds(0, N_PROTO - 1)], send.at[1])
    wait_bytes(td2.at[pl.ds(0, N_DP - 1)], send.at[2])
    wait_bytes(tp2.at[pl.ds(0, N_PROTO - 1)], send.at[3])
    wait_bytes(td3.at[pl.ds(0, N_DP - 1)], send.at[4])
    wait_bytes(rs_out.at[pl.ds(0, N_PROTO - 1)], send.at[5])
    wait_bytes(gp_out.at[pl.ds(0, N_DP - 1)], send.at[6])


def shards(
    embeddings, prototypes, embedding_log_potential, prototype_log_potential, scaled_plan_gradient
):
    rows, width = embeddings.shape
    cols = prototypes.shape[0]
    share = width // N_DP
    any_space = pl.BlockSpec(memory_space=pl.ANY)
    vmem = pl.BlockSpec(memory_space=pltpu.VMEM)
    ge, gp = pl.pallas_call(
        functools.partial(body, rows * N_DP, cols * N_PROTO),
        out_shape=(
            jax.ShapeDtypeStruct((width // N_PROTO, rows), F32),
            jax.ShapeDtypeStruct((share, cols), BF16),
        ),
        in_specs=[any_space] * 5,
        out_specs=(vmem, vmem),
        scratch_shapes=[
            pltpu.VMEM((rows, width), BF16),
            pltpu.VMEM((width, rows), BF16),
            pltpu.VMEM((cols, width), BF16),
            pltpu.VMEM((1, rows), F32),
            pltpu.VMEM((1, cols), F32),
            pltpu.VMEM((rows, cols), BF16),
            pltpu.VMEM((rows, cols), F32),
            pltpu.VMEM((rows, cols), BF16),
            pltpu.VMEM((N_DP, 2, cols), F32),
            pltpu.VMEM((N_DP, 2, cols + LANES), F32),
            pltpu.VMEM((N_DP, 8, LANES), F32),
            pltpu.VMEM((N_PROTO, 8, LANES), F32),
            pltpu.VMEM((N_PROTO, 8, LANES), F32),
            pltpu.VMEM((N_PROTO, 8, LANES), F32),
            pltpu.VMEM((N_PROTO, 8, LANES), F32),
            pltpu.VMEM((N_DP, share, cols), BF16),
            pltpu.VMEM((N_DP, share, cols), BF16),
            pltpu.SemaphoreType.DMA((5,)),
            pltpu.SemaphoreType.REGULAR,
            pltpu.SemaphoreType.DMA((7,)),
            pltpu.SemaphoreType.DMA((7,)),
        ],
        compiler_params=pltpu.CompilerParams(
            collective_id=0, has_side_effects=True, vmem_limit_bytes=56 * 1024 * 1024
        ),
    )(
        embeddings,
        prototypes,
        embedding_log_potential.reshape(1, rows),
        prototype_log_potential.reshape(1, cols),
        scaled_plan_gradient,
    )
    return ge.T, gp.T


def solution(mesh):
    return jax.shard_map(
        shards,
        mesh=mesh,
        in_specs=(P("dp", None), P("proto", None), P("dp"), P("proto"), P("dp", "proto")),
        out_specs=(P("dp", "proto"), P("proto", "dp")),
        check_vma=False,
    )
```

time: 1160 us -> 79.5 us (0.07)
  blocking collectives: 964 us -> 0 us
  waiting for transfers between devices: 136 us -> 0 us
  Pallas kernels: 0 us -> 75.7 us
  between operations: 30.8 us -> 0.64 us
    psum x12 -> x0, blocking collectives: 964 us -> none  [the longest x3 286 us: global_norm(): return lax.psum(local_inner(vector, vector), ('dp', 'proto'))]
    unnamed x3 -> x0, waiting for transfers between devices: 136 us -> none
    pallas_call x0 -> x1, Pallas kernels: none -> 75.7 us  [shards(): pl.pallas_call(functools.partial(body, rows * N_DP, cols * N_PROTO), out_...]
  transfers between devices with their start and end apart: 2 -> 0, of which waited for: 1 -> 0; matrix products, arithmetic and copies ran while one was open for 0% -> 0% of each run, Pallas kernels for 0% -> 0%
where the time goes in v1:
time: 79.5 us; the launch traced here: 79.3 us
  Pallas kernels  75.7 us (95%)
  local copies, waits for them, and re-layouts  2.95 us (4%)
    pallas_call x1, Pallas kernels, shards(): pl.pallas_call(functools.partial(body, rows * N_DP, cols * N_PROTO), out_...  75.7 us
    unnamed x2, local copies, waits for them, and re-layouts  2.95 us

profile of v1, /device:TPU:1, one launch (start us, length us, event | category | flops | bytes accessed | tf_op | source)
XLA Modules:
  0.0 79.3 jit_solution(2338758825636284556)
XLA Ops:
  0.6 75.7 %shard_map.68 = (f32[8,128]{1,0:T(8,128)}, bf16[64,2048]{1,0:T(8,128)(2,1)}) custom-call(bf16[128,512]{1,0:T(8,128)(2,1)} %e_hbm.1, bf16[2048,512]{1,0:T(8,128)(2,1)} %p_hbm.1, f32[1,128]{1,0:T(1,128)} %bitcast.7, f32[1,2048]{1,0:T(1,128)} %bitcast.5, bf16[128,2048]{1,0:T(8,128)(2,1)} %g_hbm.1), custom_call_target="tpu_custom_call" | custom-call | tf_op jit(solution)/shard_map/pallas_call | solution.py:280
  76.3 1.3 %copy.9 = f32[128,8]{0,1:T(8,128)} copy(f32[128,8]{0,1:T(8,128)} %bitcast.6) | data formatting | bytes 8192
  77.6 1.7 %copy.10 = bf16[2048,64]{0,1:T(8,128)(2,1)} copy(bf16[2048,64]{0,1:T(8,128)(2,1)} %bitcast.4) | data formatting | bytes 524288

commit v2 on v1

--- a/solution.py
+++ b/solution.py
@@ -10,6 +10,7 @@
 
 MESH = pl.DeviceIdType.MESH
 TEMP = 0.05
+EARLY = 3
 RIDGE = 0.05
 N_DP = 8
 N_Z = 8
@@ -32,8 +33,14 @@
     return jnp.sum(acc.T, axis=0, keepdims=True)
 
 
-def far_first(i):
-    return 4 + (1 - 2 * lax.rem(i, 2)) * lax.div(i + 1, 2)
+def hops(dz, dy):
+    return min(dz, N_Z - dz) + min(dy, N_Y - dy)
+
+
+FAR_FIRST = sorted(
+    [(dz, dy) for dz in range(N_Z) for dy in range(N_Y) if dz or dy], key=lambda o: -hops(*o)
+)
+DP_FAR_FIRST = (4, 5, 3, 2, 6, 1, 7)
 
 
 def wait_bytes(ref, sem):
@@ -61,7 +68,8 @@
 def body(
     rows_all, cols_all,
     e_hbm, p_hbm, er_hbm, pc_hbm, g_hbm, o_emb, o_proto,
-    ev, et, pv, er, pc, gv, kv, wv, td1, td2, td3, tp1, tp2, rs_out, rs_in, gp_out, gp_in,
+    ev, et, pv, er, pc, gv, kv, wv, td1, td2, td3, tp1, tp2, rs_out, rs_in,
+    ef, eg, erc, kf, uf, sf, sp_out, sp_own, sp_in, sx,
     in_sem, ready, send, recv,
 ):
     dp, pr = lax.axis_index("dp"), lax.axis_index("proto")
@@ -96,16 +104,14 @@
         load.wait()
 
     def to_dp(buf, i):
-        for k in range(1, N_DP):
+        for k in DP_FAR_FIRST:
             pltpu.make_async_remote_copy(
                 src_ref=buf.at[dp], dst_ref=buf.at[dp], send_sem=send.at[i], recv_sem=recv.at[i],
                 device_id=(lax.rem(dp + k, N_DP), pr), device_id_type=MESH,
             ).start()
 
     def to_proto(make, i):
-        @pl.loop(0, N_PROTO - 1)
-        def _(t):
-            dz, dy = far_first(lax.div(t, N_Y)), far_first(lax.rem(t, N_Y))
+        for dz, dy in FAR_FIRST:
             other = lax.rem(z + dz, N_Z) * N_Y + lax.rem(y + dy, N_Y)
             src, dst = make(other)
             pltpu.make_async_remote_copy(
@@ -130,6 +136,10 @@
         td1[dp, 1:2, at] = jnp.sum(w, axis=0, keepdims=True)
         row_acc += k[:, :LANES] + k[:, LANES:]
         rhs_acc += w[:, :LANES] + w[:, LANES:]
+        wv[:, at] = w.astype(BF16)
+    td1[dp, 0:1, pl.ds(cols, LANES)] = er[...]
+    td1[dp, 1:2, pl.ds(cols, LANES)] = er[...]
+    mine = pl.ds(pl.multiple_of(dp * LANES, LANES), LANES)
 
     pl.semaphore_wait(barrier, 21)
     to_dp(td1, 0)
@@ -139,12 +149,41 @@
         )
     row_part = as_row(row_acc)
     rhs_part = as_row(rhs_acc)
-    et[...] = jnp.concatenate(
-        [ev[:, j * LANES : (j + 1) * LANES].astype(F32).T for j in range(et.shape[0] // LANES)],
-        axis=0,
-    ).astype(BF16)
+
+    for j in range(N_DP // 2):
+        pair = ev[:, j * LANES : (j + 1) * LANES].astype(F32).T.astype(BF16)
+        et[2 * j] = pair[:64]
+        et[2 * j + 1] = pair[64:]
+    for k in DP_FAR_FIRST:
+        d = lax.rem(dp + k, N_DP)
+        pltpu.make_async_remote_copy(
+            src_ref=et.at[d], dst_ref=eg.at[dp], send_sem=send.at[7], recv_sem=recv.at[7],
+            device_id=(d, pr), device_id_type=MESH,
+        ).start()
+        pltpu.make_async_remote_copy(
+            src_ref=ev, dst_ref=ef.at[mine], send_sem=send.at[6], recv_sem=recv.at[6],
+            device_id=(d, pr), device_id_type=MESH,
+        ).start()
+    eg[dp] = et[dp]
+    ef[mine, :] = ev[...]
+
+    def weighted_terms(to, first):
+        lhs = jnp.concatenate([et[2 * j + first] for j in range(4)], axis=0)
+        for c in range(cols // 512):
+            at = pl.ds(c * 512, 512)
+            part = jnp.dot(lhs, wv[:, at], preferred_element_type=F32).astype(BF16)
+            for j in range(4):
+                to[j, :, at] = part[64 * j : 64 * j + 64]
+
+    x, core = lax.div(dp, 2), lax.rem(dp, 2)
+    weighted_terms(sp_out, 1 - core)
+    pltpu.make_async_remote_copy(
+        src_ref=sp_out, dst_ref=sp_in, send_sem=send.at[8], recv_sem=recv.at[8],
+        device_id=(2 * x + 1 - core, pr), device_id_type=MESH,
+    ).start()
+    weighted_terms(sp_own, core)
     wait_bytes(td1.at[pl.ds(0, N_DP - 1)], recv.at[0])
-    col_pair = jnp.sum(td1[...], axis=0)
+    col_pair = jnp.sum(td1[:, :, pl.ds(0, cols)], axis=0)
     dc = col_pair[0:1] * (1.0 / rows_all) + RIDGE
     v0c = col_pair[1:2] * (1.0 / root_rows)
 
@@ -168,6 +207,18 @@
     )
     pl.semaphore_wait(ready, 7)
     to_proto(lambda other: (tp1.at[pr], tp1.at[pr]), 1)
+
+    wait_bytes(sp_in, recv.at[8])
+    for k in (2, 1, 3):
+        other = lax.rem(x + k, 4)
+        sp_own[other] = (sp_own[other].astype(F32) + sp_in[other].astype(F32)).astype(BF16)
+        pltpu.make_async_remote_copy(
+            src_ref=sp_own.at[other], dst_ref=sx.at[x], send_sem=send.at[9], recv_sem=recv.at[9],
+            device_id=(2 * other + core, pr), device_id_type=MESH,
+        ).start()
+    sx[x] = (sp_own[x].astype(F32) + sp_in[x].astype(F32)).astype(BF16)
+    for d in range(N_DP):
+        erc[d * LANES : (d + 1) * LANES, :] = as_column(td1[d, 0:1, cols:])
     wait_bytes(tp1.at[pl.ds(0, N_PROTO - 1)], recv.at[1])
     one = jnp.sum(tp1[...], axis=0)
     dr = one[0:1] * (1.0 / cols_all) + RIDGE
@@ -184,11 +235,26 @@
         td2[dp, 1:2, at] = jnp.sum(k * p_col, axis=0, keepdims=True)
     td2[dp, 0:1, pl.ds(cols, LANES)] = v0r * v0r
     td2[dp, 1:2, pl.ds(cols, LANES)] = v0r * (dr * v0r + (2.0 * coupling) * kv0)
+    td2[dp, 0:1, pl.ds(cols + LANES, LANES)] = v0r
+    td2[dp, 1:2, pl.ds(cols + LANES, LANES)] = p_r
     to_dp(td2, 2)
+
+    def whole_kernel(c):
+        at = pl.ds(c * wide, wide)
+        scores = lax.dot_general(
+            ef[...], pv[at, :], (((1,), (1,)), ((), ())), preferred_element_type=F32
+        )
+        shift = jnp.concatenate([erc[...], erc[...]], axis=1)
+        kf[:, at] = jnp.exp(scores * (1.0 / TEMP) + shift + pc[:, at]).astype(BF16)
+
+    wait_bytes(ef.at[pl.ds(0, (N_DP - 1) * LANES)], recv.at[6])
+    wait_bytes(eg.at[pl.ds(0, N_DP - 1)], recv.at[7])
+    for c in range(EARLY):
+        whole_kernel(c)
     wait_bytes(td2.at[pl.ds(0, N_DP - 1)], recv.at[2])
     two = jnp.sum(td2[...], axis=0)
-    m0 = s0 + total(two[0:1, cols:])
-    m1 = s1 + total(two[1:2, cols:])
+    m0 = s0 + total(two[0:1, cols : cols + LANES])
+    m1 = s1 + total(two[1:2, cols : cols + LANES])
     theta = m1 / m0
     step = m0 / m1
     ktv0, ktp = two[0:1, :cols], two[1:2, :cols]
@@ -204,16 +270,29 @@
         axis=0,
     )
     to_proto(lambda other: (tp2.at[pr], tp2.at[pr]), 3)
+    for c in range(EARLY, cols // wide):
+        whole_kernel(c)
+    lhs = jnp.concatenate([eg[d] for d in range(N_DP)], axis=1)
+    for c in range(cols // 512):
+        at = pl.ds(c * 512, 512)
+        uf[:, at] = jnp.dot(lhs, kf[:, at], preferred_element_type=F32)
     wait_bytes(tp2.at[pl.ds(0, N_PROTO - 1)], recv.at[3])
     three = jnp.sum(tp2[...], axis=0)
     kr1, kw = three[0:1], three[1:2]
     wr = step * (dr * r1r + coupling * kr1) - r1r
     td3[dp] = jnp.concatenate(
         [r1r * r1r, r1r * wr, v0r * wr, wr * wr, wr * (dr * wr + (2.0 * coupling) * kw), v0r * r1r,
-         jnp.zeros((2, LANES), F32)],
+         wr, jnp.zeros((1, LANES), F32)],
         axis=0,
     )
     to_dp(td3, 4)
+    wait_bytes(sx.at[pl.ds(0, 3)], recv.at[9])
+    for c in range(cols // 512):
+        at = pl.ds(c * 512, 512)
+        acc = sx[0, :, at].astype(F32)
+        for j in range(1, 4):
+            acc += sx[j, :, at].astype(F32)
+        sf[:, at] = acc
     wait_bytes(td3.at[pl.ds(0, N_DP - 1)], recv.at[4])
     four = total(jnp.sum(td3[...], axis=0))
     five = total(three)
@@ -237,28 +316,20 @@
     to_proto(lambda other: (rs_out.at[other], rs_in.at[pr]), 5)
     rs_in[pr] = rs_out[pr]
 
-    def proto_terms(d):
-        part = et[pl.ds(pl.multiple_of(d * 64, 64), 64), :]
-        gp_out[d] = jnp.dot(part, wv[...], preferred_element_type=F32).astype(BF16)
-
-    for k in range(1, N_DP):
-        d = lax.rem(dp + k, N_DP)
-        proto_terms(d)
-        pltpu.make_async_remote_copy(
-            src_ref=gp_out.at[d], dst_ref=gp_in.at[dp], send_sem=send.at[6], recv_sem=recv.at[6],
-            device_id=(d, pr), device_id_type=MESH,
-        ).start()
-    proto_terms(dp)
-    gp_in[dp] = gp_out[dp]
+    scaled = []
+    for d in range(N_DP):
+        v0d = td2[d, 0:1, pl.ds(cols + LANES, LANES)]
+        r1d = v0d - step * td2[d, 1:2, pl.ds(cols + LANES, LANES)]
+        sol_d = (y0 * v0d + y1 * r1d + y2 * td3[d, 6:7, :]) * (1.0 / root_cols)
+        scaled.append((eg[d].astype(F32) * sol_d).astype(BF16))
+    lhs = jnp.concatenate(scaled, axis=1)
+    for c in range(cols // 512):
+        at = pl.ds(c * 512, 512)
+        terms = jnp.dot(lhs, kf[:, at], preferred_element_type=F32)
+        part = sf[:, at] - terms - uf[:, at] * sol_c[:, c * 512 : (c + 1) * 512]
+        o_proto[:, at] = (part * (1.0 / TEMP)).astype(BF16)
     wait_bytes(rs_in.at[pl.ds(0, N_PROTO - 1)], recv.at[5])
     o_emb[...] = jnp.sum(rs_in[...], axis=0)
-    wait_bytes(gp_in.at[pl.ds(0, N_DP - 1)], recv.at[6])
-    for c in range(cols // 512):
-        at = pl.ds(c * 512, 512)
-        acc = gp_in[0, :, at].astype(F32)
-        for d in range(1, N_DP):
-            acc += gp_in[d, :, at].astype(F32)
-        o_proto[:, at] = acc.astype(BF16)
 
     wait_bytes(td1.at[pl.ds(0, N_DP - 1)], send.at[0])
     wait_bytes(tp1.at[pl.ds(0, N_PROTO - 1)], send.at[1])
@@ -266,7 +337,10 @@
     wait_bytes(tp2.at[pl.ds(0, N_PROTO - 1)], send.at[3])
     wait_bytes(td3.at[pl.ds(0, N_DP - 1)], send.at[4])
     wait_bytes(rs_out.at[pl.ds(0, N_PROTO - 1)], send.at[5])
-    wait_bytes(gp_out.at[pl.ds(0, N_DP - 1)], send.at[6])
+    wait_bytes(ef.at[pl.ds(0, (N_DP - 1) * LANES)], send.at[6])
+    wait_bytes(et.at[pl.ds(0, N_DP - 1)], send.at[7])
+    wait_bytes(sp_out, send.at[8])
+    wait_bytes(sp_own.at[pl.ds(0, 3)], send.at[9])
 
 
 def shards(
@@ -287,26 +361,34 @@
         out_specs=(vmem, vmem),
         scratch_shapes=[
             pltpu.VMEM((rows, width), BF16),
-            pltpu.VMEM((width, rows), BF16),
+            pltpu.VMEM((N_DP, share, rows), BF16),
             pltpu.VMEM((cols, width), BF16),
             pltpu.VMEM((1, rows), F32),
             pltpu.VMEM((1, cols), F32),
             pltpu.VMEM((rows, cols), BF16),
             pltpu.VMEM((rows, cols), F32),
             pltpu.VMEM((rows, cols), BF16),
-            pltpu.VMEM((N_DP, 2, cols), F32),
             pltpu.VMEM((N_DP, 2, cols + LANES), F32),
+            pltpu.VMEM((N_DP, 2, cols + 2 * LANES), F32),
             pltpu.VMEM((N_DP, 8, LANES), F32),
             pltpu.VMEM((N_PROTO, 8, LANES), F32),
             pltpu.VMEM((N_PROTO, 8, LANES), F32),
             pltpu.VMEM((N_PROTO, 8, LANES), F32),
             pltpu.VMEM((N_PROTO, 8, LANES), F32),
-            pltpu.VMEM((N_DP, share, cols), BF16),
-            pltpu.VMEM((N_DP, share, cols), BF16),
+            pltpu.VMEM((rows * N_DP, width), BF16),
+            pltpu.VMEM((N_DP, share, rows), BF16),
+            pltpu.VMEM((rows * N_DP, LANES), F32),
+            pltpu.VMEM((rows * N_DP, cols), BF16),
+            pltpu.VMEM((share, cols), F32),
+            pltpu.VMEM((share, cols), F32),
+            pltpu.VMEM((4, share, cols), BF16),
+            pltpu.VMEM((4, share, cols), BF16),
+            pltpu.VMEM((4, share, cols), BF16),
+            pltpu.VMEM((4, share, cols), BF16),
             pltpu.SemaphoreType.DMA((5,)),
             pltpu.SemaphoreType.REGULAR,
-            pltpu.SemaphoreType.DMA((7,)),
-            pltpu.SemaphoreType.DMA((7,)),
+            pltpu.SemaphoreType.DMA((10,)),
+            pltpu.SemaphoreType.DMA((10,)),
         ],
         compiler_params=pltpu.CompilerParams(
             collective_id=0, has_side_effects=True, vmem_limit_bytes=56 * 1024 * 1024

time: 79.5 us -> 71.6 us (0.901)
  Pallas kernels: 75.7 us -> 67.8 us
    pallas_call x1, Pallas kernels: 75.7 us -> 67.8 us  [shards(): pl.pallas_call(functools.partial(body, rows * N_DP, cols * N_PROTO), out_...]
where the time goes in v2:
time: 71.6 us; the launch traced here: 71.4 us
  Pallas kernels  67.8 us (95%)
  local copies, waits for them, and re-layouts  2.95 us (4%)
    pallas_call x1, Pallas kernels, shards(): pl.pallas_call(functools.partial(body, rows * N_DP, cols * N_PROTO), out_...  67.8 us
    unnamed x2, local copies, waits for them, and re-layouts  2.95 us

profile of v2, /device:TPU:1, one launch (start us, length us, event | category | flops | bytes accessed | tf_op | source)
XLA Modules:
  0.0 71.4 jit_solution(14331152721252704614)
XLA Ops:
  0.6 67.8 %shard_map.68 = (f32[8,128]{1,0:T(8,128)}, bf16[64,2048]{1,0:T(8,128)(2,1)}) custom-call(bf16[128,512]{1,0:T(8,128)(2,1)} %e_hbm.1, bf16[2048,512]{1,0:T(8,128)(2,1)} %p_hbm.1, f32[1,128]{1,0:T(1,128)} %bitcast.7, f32[1,2048]{1,0:T(1,128)} %bitcast.5, bf16[128,2048]{1,0:T(8,128)(2,1)} %g_hbm.1), custom_call_target="tpu_custom_call" | custom-call | tf_op jit(solution)/shard_map/pallas_call | solution.py:354
  68.5 1.3 %copy.9 = f32[128,8]{0,1:T(8,128)} copy(f32[128,8]{0,1:T(8,128)} %bitcast.6) | data formatting | bytes 8192
  69.8 1.7 %copy.10 = bf16[2048,64]{0,1:T(8,128)(2,1)} copy(bf16[2048,64]{0,1:T(8,128)(2,1)} %bitcast.4) | data formatting | bytes 524288

commit v3 on v2

--- a/solution.py
+++ b/solution.py
@@ -10,7 +10,6 @@
 
 MESH = pl.DeviceIdType.MESH
 TEMP = 0.05
-EARLY = 3
 RIDGE = 0.05
 N_DP = 8
 N_Z = 8
@@ -136,7 +135,6 @@
         td1[dp, 1:2, at] = jnp.sum(w, axis=0, keepdims=True)
         row_acc += k[:, :LANES] + k[:, LANES:]
         rhs_acc += w[:, :LANES] + w[:, LANES:]
-        wv[:, at] = w.astype(BF16)
     td1[dp, 0:1, pl.ds(cols, LANES)] = er[...]
     td1[dp, 1:2, pl.ds(cols, LANES)] = er[...]
     mine = pl.ds(pl.multiple_of(dp * LANES, LANES), LANES)
@@ -154,18 +152,59 @@
         pair = ev[:, j * LANES : (j + 1) * LANES].astype(F32).T.astype(BF16)
         et[2 * j] = pair[:64]
         et[2 * j + 1] = pair[64:]
-    for k in DP_FAR_FIRST:
-        d = lax.rem(dp + k, N_DP)
+    wait_bytes(td1.at[pl.ds(0, N_DP - 1)], recv.at[0])
+    col_pair = jnp.sum(td1[:, :, pl.ds(0, cols)], axis=0)
+    dc = col_pair[0:1] * (1.0 / rows_all) + RIDGE
+    v0c = col_pair[1:2] * (1.0 / root_rows)
+
+    def lanes(row, t):
+        return row[:, t * LANES : (t + 1) * LANES]
+
+    def fold(row):
+        return functools.reduce(lambda a, b: a + b, [lanes(row, t) for t in range(tiles)])
+
+    def k_times(*vectors):
+        accs = [jnp.zeros((LANES, LANES), F32) for _ in vectors]
+        for t in range(tiles):
+            k = kv[:, t * LANES : (t + 1) * LANES]
+            accs = [a + k * lanes(v, t) for a, v in zip(accs, vectors)]
+        return [as_row(a) for a in accs]
+
+    (kv0,) = k_times(v0c)
+    lane = lax.broadcasted_iota(jnp.int32, (1, LANES), 1)
+
+    def by_two(row):
+        return row + pltpu.roll(row, 64, 1)
+
+    def by_four(row):
+        row = by_two(row)
+        return row + pltpu.roll(row, 32, 1)
+
+    tp1[pr] = jnp.concatenate(
+        [row_part, rhs_part, kv0,
+         jnp.where(lane < 64, by_two(fold(v0c * v0c)), by_two(fold(v0c * dc * v0c)))],
+        axis=0,
+    )
+    pl.semaphore_wait(ready, 7)
+    to_proto(lambda other: (tp1.at[pr], tp1.at[pr]), 1)
+
+    x, core = lax.div(dp, 2), lax.rem(dp, 2)
+    sibling = 2 * x + 1 - core
+
+    def block(d):
+        return ef.at[pl.ds(pl.multiple_of(d * LANES, LANES), LANES)]
+
+    for k in (2, 1, 3):
         pltpu.make_async_remote_copy(
-            src_ref=et.at[d], dst_ref=eg.at[dp], send_sem=send.at[7], recv_sem=recv.at[7],
-            device_id=(d, pr), device_id_type=MESH,
+            src_ref=ev, dst_ref=block(dp), send_sem=send.at[6], recv_sem=recv.at[6],
+            device_id=(2 * lax.rem(x + k, 4) + core, pr), device_id_type=MESH,
         ).start()
-        pltpu.make_async_remote_copy(
-            src_ref=ev, dst_ref=ef.at[mine], send_sem=send.at[6], recv_sem=recv.at[6],
-            device_id=(d, pr), device_id_type=MESH,
-        ).start()
-    eg[dp] = et[dp]
     ef[mine, :] = ev[...]
+
+    guess = col_pair[1:2] * (1.0 / rows_all) / dc
+    for t in range(tiles):
+        at = pl.ds(t * LANES, LANES)
+        wv[:, at] = (kv[:, at] * (gv[:, at].astype(F32) - lanes(guess, t))).astype(BF16)
 
     def weighted_terms(to, first):
         lhs = jnp.concatenate([et[2 * j + first] for j in range(4)], axis=0)
@@ -175,48 +214,12 @@
             for j in range(4):
                 to[j, :, at] = part[64 * j : 64 * j + 64]
 
-    x, core = lax.div(dp, 2), lax.rem(dp, 2)
     weighted_terms(sp_out, 1 - core)
     pltpu.make_async_remote_copy(
         src_ref=sp_out, dst_ref=sp_in, send_sem=send.at[8], recv_sem=recv.at[8],
-        device_id=(2 * x + 1 - core, pr), device_id_type=MESH,
+        device_id=(sibling, pr), device_id_type=MESH,
     ).start()
     weighted_terms(sp_own, core)
-    wait_bytes(td1.at[pl.ds(0, N_DP - 1)], recv.at[0])
-    col_pair = jnp.sum(td1[:, :, pl.ds(0, cols)], axis=0)
-    dc = col_pair[0:1] * (1.0 / rows_all) + RIDGE
-    v0c = col_pair[1:2] * (1.0 / root_rows)
-
-    def lanes(row, t):
-        return row[:, t * LANES : (t + 1) * LANES]
-
-    def fold(row):
-        return functools.reduce(lambda a, b: a + b, [lanes(row, t) for t in range(tiles)])
-
-    def k_times(*vectors):
-        accs = [jnp.zeros((LANES, LANES), F32) for _ in vectors]
-        for t in range(tiles):
-            k = kv[:, t * LANES : (t + 1) * LANES]
-            accs = [a + k * lanes(v, t) for a, v in zip(accs, vectors)]
-        return [as_row(a) for a in accs]
-
-    (kv0,) = k_times(v0c)
-    tp1[pr] = jnp.concatenate(
-        [row_part, rhs_part, kv0, fold(v0c * v0c), fold(v0c * dc * v0c), jnp.zeros((3, LANES), F32)],
-        axis=0,
-    )
-    pl.semaphore_wait(ready, 7)
-    to_proto(lambda other: (tp1.at[pr], tp1.at[pr]), 1)
-
-    wait_bytes(sp_in, recv.at[8])
-    for k in (2, 1, 3):
-        other = lax.rem(x + k, 4)
-        sp_own[other] = (sp_own[other].astype(F32) + sp_in[other].astype(F32)).astype(BF16)
-        pltpu.make_async_remote_copy(
-            src_ref=sp_own.at[other], dst_ref=sx.at[x], send_sem=send.at[9], recv_sem=recv.at[9],
-            device_id=(2 * other + core, pr), device_id_type=MESH,
-        ).start()
-    sx[x] = (sp_own[x].astype(F32) + sp_in[x].astype(F32)).astype(BF16)
     for d in range(N_DP):
         erc[d * LANES : (d + 1) * LANES, :] = as_column(td1[d, 0:1, cols:])
     wait_bytes(tp1.at[pl.ds(0, N_PROTO - 1)], recv.at[1])
@@ -224,7 +227,8 @@
     dr = one[0:1] * (1.0 / cols_all) + RIDGE
     v0r = one[1:2] * (1.0 / root_cols)
     kv0 = one[2:3]
-    s0, s1 = total(one[3:4]), total(one[4:5])
+    s0 = total(jnp.where(lane < 64, one[3:4], 0.0))
+    s1 = total(jnp.where(lane < 64, 0.0, one[3:4]))
     p_r = dr * v0r + coupling * kv0
 
     v0_col, p_col = as_column(v0r), as_column(p_r)
@@ -247,10 +251,16 @@
         shift = jnp.concatenate([erc[...], erc[...]], axis=1)
         kf[:, at] = jnp.exp(scores * (1.0 / TEMP) + shift + pc[:, at]).astype(BF16)
 
-    wait_bytes(ef.at[pl.ds(0, (N_DP - 1) * LANES)], recv.at[6])
-    wait_bytes(eg.at[pl.ds(0, N_DP - 1)], recv.at[7])
-    for c in range(EARLY):
-        whole_kernel(c)
+    wait_bytes(ef.at[pl.ds(0, 3 * LANES)], recv.at[6])
+    for j in range(4):
+        pltpu.make_async_remote_copy(
+            src_ref=block(2 * j + core), dst_ref=block(2 * j + core),
+            send_sem=send.at[7], recv_sem=recv.at[7],
+            device_id=(sibling, pr), device_id_type=MESH,
+        ).start()
+    wait_bytes(sp_in, recv.at[8])
+    for j in range(4):
+        sp_own[j] = (sp_own[j].astype(F32) + sp_in[j].astype(F32)).astype(BF16)
     wait_bytes(td2.at[pl.ds(0, N_DP - 1)], recv.at[2])
     two = jnp.sum(td2[...], axis=0)
     m0 = s0 + total(two[0:1, cols : cols + LANES])
@@ -264,15 +274,29 @@
     wc = step * (dc * r1c + coupling * ktr1) - r1c
 
     kr1, kw = k_times(r1c, wc)
+    q = [by_four(fold(v)) for v in
+         (r1c * r1c, r1c * wc, v0c * wc, wc * wc, wc * dc * wc, v0c * r1c)]
     tp2[pr] = jnp.concatenate(
-        [kr1, kw, fold(r1c * r1c), fold(r1c * wc), fold(v0c * wc), fold(wc * wc),
-         fold(wc * dc * wc), fold(v0c * r1c)],
+        [kr1, kw,
+         jnp.where(lane < 64, jnp.where(lane < 32, q[0], q[1]), jnp.where(lane < 96, q[2], q[3])),
+         jnp.where(lane < 64, jnp.where(lane < 32, q[4], q[5]), 0.0)],
         axis=0,
     )
     to_proto(lambda other: (tp2.at[pr], tp2.at[pr]), 3)
-    for c in range(EARLY, cols // wide):
+    for k in (2, 1, 3):
+        other = lax.rem(x + k, 4)
+        pltpu.make_async_remote_copy(
+            src_ref=sp_own.at[other], dst_ref=sx.at[x], send_sem=send.at[9], recv_sem=recv.at[9],
+            device_id=(2 * other + core, pr), device_id_type=MESH,
+        ).start()
+    sx[x] = sp_own[x]
+    wait_bytes(ef.at[pl.ds(0, 4 * LANES)], recv.at[7])
+    for d in range(N_DP):
+        eg[d] = ef[d * LANES : (d + 1) * LANES, pl.ds(pl.multiple_of(x * LANES, LANES), LANES)].astype(F32).T
+    for c in range(cols // wide):
         whole_kernel(c)
-    lhs = jnp.concatenate([eg[d] for d in range(N_DP)], axis=1)
+    share = pl.ds(pl.multiple_of(64 * core, 64), 64)
+    lhs = jnp.concatenate([eg[d, share, :] for d in range(N_DP)], axis=1).astype(BF16)
     for c in range(cols // 512):
         at = pl.ds(c * 512, 512)
         uf[:, at] = jnp.dot(lhs, kf[:, at], preferred_element_type=F32)
@@ -295,11 +319,12 @@
         sf[:, at] = acc
     wait_bytes(td3.at[pl.ds(0, N_DP - 1)], recv.at[4])
     four = total(jnp.sum(td3[...], axis=0))
-    five = total(three)
-    r1r1, r1w = four[0:1] + five[2:3], four[1:2] + five[3:4]
-    v0w, ww = four[2:3] + five[4:5], four[3:4] + five[5:6]
-    waw = (four[4:5] + five[6:7]) * step
-    v0r1 = four[5:6] + five[7:8]
+    five = [
+        total(jnp.where((lane >= 32 * g) & (lane < 32 * g + 32), three[r : r + 1], 0.0))
+        for r, g in ((2, 0), (2, 1), (2, 2), (2, 3), (3, 0), (3, 1))
+    ]
+    r1r1, r1w, v0w = four[0:1] + five[0], four[1:2] + five[1], four[2:3] + five[2]
+    ww, waw, v0r1 = four[3:4] + five[3], (four[4:5] + five[4]) * step, four[5:6] + five[5]
     y0, y1, y2 = solve(m0, v0r1, v0w, r1r1, r1w, ww, waw)
     y0, y1, y2 = y0 * step, y1 * step, y2 * step
     sol_r = (y0 * v0r + y1 * r1r + y2 * wr) * (1.0 / root_cols)
@@ -312,7 +337,7 @@
         wv[:, at] = (kv[:, at] * (g - sol_col - lanes(sol_c, t)) * (1.0 / TEMP)).astype(BF16)
     ge = jnp.dot(wv[...], pv[...], preferred_element_type=F32)
     for j in range(4):
-        rs_out[pl.ds(16 * j, 16)] = ge[:, j * LANES : (j + 1) * LANES].T.reshape(16, 8, LANES)
+        rs_out[pl.ds(16 * j, 16)] = ge[:, j * LANES : (j + 1) * LANES].T.reshape(16, 8, LANES).astype(BF16)
     to_proto(lambda other: (rs_out.at[other], rs_in.at[pr]), 5)
     rs_in[pr] = rs_out[pr]
 
@@ -321,15 +346,15 @@
         v0d = td2[d, 0:1, pl.ds(cols + LANES, LANES)]
         r1d = v0d - step * td2[d, 1:2, pl.ds(cols + LANES, LANES)]
         sol_d = (y0 * v0d + y1 * r1d + y2 * td3[d, 6:7, :]) * (1.0 / root_cols)
-        scaled.append((eg[d].astype(F32) * sol_d).astype(BF16))
+        scaled.append((eg[d, share, :] * sol_d).astype(BF16))
     lhs = jnp.concatenate(scaled, axis=1)
     for c in range(cols // 512):
         at = pl.ds(c * 512, 512)
         terms = jnp.dot(lhs, kf[:, at], preferred_element_type=F32)
-        part = sf[:, at] - terms - uf[:, at] * sol_c[:, c * 512 : (c + 1) * 512]
+        part = sf[:, at] - terms - uf[:, at] * (sol_c - guess)[:, c * 512 : (c + 1) * 512]
         o_proto[:, at] = (part * (1.0 / TEMP)).astype(BF16)
     wait_bytes(rs_in.at[pl.ds(0, N_PROTO - 1)], recv.at[5])
-    o_emb[...] = jnp.sum(rs_in[...], axis=0)
+    o_emb[...] = jnp.sum(rs_in[...].astype(F32), axis=0)
 
     wait_bytes(td1.at[pl.ds(0, N_DP - 1)], send.at[0])
     wait_bytes(tp1.at[pl.ds(0, N_PROTO - 1)], send.at[1])
@@ -337,8 +362,8 @@
     wait_bytes(tp2.at[pl.ds(0, N_PROTO - 1)], send.at[3])
     wait_bytes(td3.at[pl.ds(0, N_DP - 1)], send.at[4])
     wait_bytes(rs_out.at[pl.ds(0, N_PROTO - 1)], send.at[5])
-    wait_bytes(ef.at[pl.ds(0, (N_DP - 1) * LANES)], send.at[6])
-    wait_bytes(et.at[pl.ds(0, N_DP - 1)], send.at[7])
+    wait_bytes(ef.at[pl.ds(0, 3 * LANES)], send.at[6])
+    wait_bytes(ef.at[pl.ds(0, 4 * LANES)], send.at[7])
     wait_bytes(sp_out, send.at[8])
     wait_bytes(sp_own.at[pl.ds(0, 3)], send.at[9])
 
@@ -371,12 +396,12 @@
             pltpu.VMEM((N_DP, 2, cols + LANES), F32),
             pltpu.VMEM((N_DP, 2, cols + 2 * LANES), F32),
             pltpu.VMEM((N_DP, 8, LANES), F32),
-            pltpu.VMEM((N_PROTO, 8, LANES), F32),
-            pltpu.VMEM((N_PROTO, 8, LANES), F32),
-            pltpu.VMEM((N_PROTO, 8, LANES), F32),
-            pltpu.VMEM((N_PROTO, 8, LANES), F32),
+            pltpu.VMEM((N_PROTO, 4, LANES), F32),
+            pltpu.VMEM((N_PROTO, 4, LANES), F32),
+            pltpu.VMEM((N_PROTO, 8, LANES), BF16),
+            pltpu.VMEM((N_PROTO, 8, LANES), BF16),
             pltpu.VMEM((rows * N_DP, width), BF16),
-            pltpu.VMEM((N_DP, share, rows), BF16),
+            pltpu.VMEM((N_DP, LANES, rows), F32),
             pltpu.VMEM((rows * N_DP, LANES), F32),
             pltpu.VMEM((rows * N_DP, cols), BF16),
             pltpu.VMEM((share, cols), F32),

time: 71.6 us -> 57.4 us (0.80)
  Pallas kernels: 67.8 us -> 53.6 us
    pallas_call x1, Pallas kernels: 67.8 us -> 53.6 us  [shards(): pl.pallas_call(functools.partial(body, rows * N_DP, cols * N_PROTO), out_...]
where the time goes in v3:
time: 57.4 us; the launch traced here: 57.2 us
  Pallas kernels  53.6 us (93%)
  local copies, waits for them, and re-layouts  2.95 us (5%)
  between operations  0.64 us (1%)
    pallas_call x1, Pallas kernels, shards(): pl.pallas_call(functools.partial(body, rows * N_DP, cols * N_PROTO), out_...  53.6 us
    unnamed x2, local copies, waits for them, and re-layouts  2.95 us

profile of v3, /device:TPU:1, one launch (start us, length us, event | category | flops | bytes accessed | tf_op | source)
XLA Modules:
  0.0 57.2 jit_solution(6757087517591223098)
XLA Ops:
  0.6 53.6 %shard_map.68 = (f32[8,128]{1,0:T(8,128)}, bf16[64,2048]{1,0:T(8,128)(2,1)}) custom-call(bf16[128,512]{1,0:T(8,128)(2,1)} %e_hbm.1, bf16[2048,512]{1,0:T(8,128)(2,1)} %p_hbm.1, f32[1,128]{1,0:T(1,128)} %bitcast.7, f32[1,2048]{1,0:T(1,128)} %bitcast.5, bf16[128,2048]{1,0:T(8,128)(2,1)} %g_hbm.1), custom_call_target="tpu_custom_call" | custom-call | tf_op jit(solution)/shard_map/pallas_call | solution.py:379
  54.3 1.3 %copy.9 = f32[128,8]{0,1:T(8,128)} copy(f32[128,8]{0,1:T(8,128)} %bitcast.6) | data formatting | bytes 8192
  55.5 1.7 %copy.10 = bf16[2048,64]{0,1:T(8,128)(2,1)} copy(bf16[2048,64]{0,1:T(8,128)(2,1)} %bitcast.4) | data formatting | bytes 524288

commit v4 on v3

--- a/solution.py
+++ b/solution.py
@@ -68,7 +68,7 @@
     rows_all, cols_all,
     e_hbm, p_hbm, er_hbm, pc_hbm, g_hbm, o_emb, o_proto,
     ev, et, pv, er, pc, gv, kv, wv, td1, td2, td3, tp1, tp2, rs_out, rs_in,
-    ef, eg, erc, kf, uf, sf, sp_out, sp_own, sp_in, sx,
+    ef, eg, erc, kf, uf, sf, sp_out, sp_own, sp_in, s2, sx,
     in_sem, ready, send, recv,
 ):
     dp, pr = lax.axis_index("dp"), lax.axis_index("proto")
@@ -261,6 +261,13 @@
     wait_bytes(sp_in, recv.at[8])
     for j in range(4):
         sp_own[j] = (sp_own[j].astype(F32) + sp_in[j].astype(F32)).astype(BF16)
+    right, left, across = (lax.rem(x + k, 4) for k in (1, 3, 2))
+    for i, to in enumerate((right, left)):
+        pltpu.make_async_remote_copy(
+            src_ref=sp_own.at[across, pl.ds(32 * i, 32)], dst_ref=s2.at[i],
+            send_sem=send.at[9], recv_sem=recv.at[9],
+            device_id=(2 * to + core, pr), device_id_type=MESH,
+        ).start()
     wait_bytes(td2.at[pl.ds(0, N_DP - 1)], recv.at[2])
     two = jnp.sum(td2[...], axis=0)
     m0 = s0 + total(two[0:1, cols : cols + LANES])
@@ -283,13 +290,14 @@
         axis=0,
     )
     to_proto(lambda other: (tp2.at[pr], tp2.at[pr]), 3)
-    for k in (2, 1, 3):
-        other = lax.rem(x + k, 4)
+    wait_bytes(s2, recv.at[9])
+    for i, to in enumerate((right, left)):
+        half = pl.ds(32 * i, 32)
+        sp_own[to, half] = (sp_own[to, half].astype(F32) + s2[i].astype(F32)).astype(BF16)
         pltpu.make_async_remote_copy(
-            src_ref=sp_own.at[other], dst_ref=sx.at[x], send_sem=send.at[9], recv_sem=recv.at[9],
-            device_id=(2 * other + core, pr), device_id_type=MESH,
+            src_ref=sp_own.at[to], dst_ref=sx.at[i], send_sem=send.at[10], recv_sem=recv.at[10],
+            device_id=(2 * to + core, pr), device_id_type=MESH,
         ).start()
-    sx[x] = sp_own[x]
     wait_bytes(ef.at[pl.ds(0, 4 * LANES)], recv.at[7])
     for d in range(N_DP):
         eg[d] = ef[d * LANES : (d + 1) * LANES, pl.ds(pl.multiple_of(x * LANES, LANES), LANES)].astype(F32).T
@@ -310,27 +318,21 @@
         axis=0,
     )
     to_dp(td3, 4)
-    wait_bytes(sx.at[pl.ds(0, 3)], recv.at[9])
-    for c in range(cols // 512):
-        at = pl.ds(c * 512, 512)
-        acc = sx[0, :, at].astype(F32)
-        for j in range(1, 4):
-            acc += sx[j, :, at].astype(F32)
-        sf[:, at] = acc
-    wait_bytes(td3.at[pl.ds(0, N_DP - 1)], recv.at[4])
-    four = total(jnp.sum(td3[...], axis=0))
     five = [
         total(jnp.where((lane >= 32 * g) & (lane < 32 * g + 32), three[r : r + 1], 0.0))
         for r, g in ((2, 0), (2, 1), (2, 2), (2, 3), (3, 0), (3, 1))
     ]
+    sol_cols = [as_column(v) for v in (v0r, r1r, wr)]
+    wait_bytes(td3.at[pl.ds(0, N_DP - 1)], recv.at[4])
+    four = total(jnp.sum(td3[...], axis=0))
     r1r1, r1w, v0w = four[0:1] + five[0], four[1:2] + five[1], four[2:3] + five[2]
     ww, waw, v0r1 = four[3:4] + five[3], (four[4:5] + five[4]) * step, four[5:6] + five[5]
     y0, y1, y2 = solve(m0, v0r1, v0w, r1r1, r1w, ww, waw)
     y0, y1, y2 = y0 * step, y1 * step, y2 * step
-    sol_r = (y0 * v0r + y1 * r1r + y2 * wr) * (1.0 / root_cols)
     sol_c = (y0 * v0c + y1 * r1c + y2 * wc) * (1.0 / root_rows)
 
-    sol_col = as_column(sol_r)
+    ys = [v * (1.0 / root_cols) for v in (y0, y1, y2)]
+    sol_col = ys[0] * sol_cols[0] + ys[1] * sol_cols[1] + ys[2] * sol_cols[2]
     for t in range(tiles):
         at = pl.ds(t * LANES, LANES)
         g = gv[:, at].astype(F32)
@@ -340,6 +342,11 @@
         rs_out[pl.ds(16 * j, 16)] = ge[:, j * LANES : (j + 1) * LANES].T.reshape(16, 8, LANES).astype(BF16)
     to_proto(lambda other: (rs_out.at[other], rs_in.at[pr]), 5)
     rs_in[pr] = rs_out[pr]
+    wait_bytes(sx, recv.at[10])
+    for c in range(cols // 512):
+        at = pl.ds(c * 512, 512)
+        both = sx[0, :, at].astype(F32) + sx[1, :, at].astype(F32)
+        sf[:, at] = sp_own[x, :, at].astype(F32) + both
 
     scaled = []
     for d in range(N_DP):
@@ -365,7 +372,8 @@
     wait_bytes(ef.at[pl.ds(0, 3 * LANES)], send.at[6])
     wait_bytes(ef.at[pl.ds(0, 4 * LANES)], send.at[7])
     wait_bytes(sp_out, send.at[8])
-    wait_bytes(sp_own.at[pl.ds(0, 3)], send.at[9])
+    wait_bytes(s2, send.at[9])
+    wait_bytes(sx, send.at[10])
 
 
 def shards(
@@ -409,11 +417,12 @@
             pltpu.VMEM((4, share, cols), BF16),
             pltpu.VMEM((4, share, cols), BF16),
             pltpu.VMEM((4, share, cols), BF16),
-            pltpu.VMEM((4, share, cols), BF16),
+            pltpu.VMEM((2, share // 2, cols), BF16),
+            pltpu.VMEM((2, share, cols), BF16),
             pltpu.SemaphoreType.DMA((5,)),
             pltpu.SemaphoreType.REGULAR,
-            pltpu.SemaphoreType.DMA((10,)),
-            pltpu.SemaphoreType.DMA((10,)),
+            pltpu.SemaphoreType.DMA((11,)),
+            pltpu.SemaphoreType.DMA((11,)),
         ],
         compiler_params=pltpu.CompilerParams(
             collective_id=0, has_side_effects=True, vmem_limit_bytes=56 * 1024 * 1024

time: 57.4 us -> 53.8 us (0.937)
  Pallas kernels: 53.6 us -> 50 us
    pallas_call x1, Pallas kernels: 53.6 us -> 50 us  [shards(): pl.pallas_call(functools.partial(body, rows * N_DP, cols * N_PROTO), out_...]
where the time goes in v4:
time: 53.8 us; the launch traced here: 53.5 us
  Pallas kernels  50 us (93%)
  local copies, waits for them, and re-layouts  2.95 us (5%)
  between operations  0.64 us (1%)
    pallas_call x1, Pallas kernels, shards(): pl.pallas_call(functools.partial(body, rows * N_DP, cols * N_PROTO), out_...  50 us
    unnamed x2, local copies, waits for them, and re-layouts  2.95 us

profile of v4, /device:TPU:1, one launch (start us, length us, event | category | flops | bytes accessed | tf_op | source)
XLA Modules:
  0.0 53.5 jit_solution(5050435463326083566)
XLA Ops:
  0.6 50.0 %shard_map.68 = (f32[8,128]{1,0:T(8,128)}, bf16[64,2048]{1,0:T(8,128)(2,1)}) custom-call(bf16[128,512]{1,0:T(8,128)(2,1)} %e_hbm.1, bf16[2048,512]{1,0:T(8,128)(2,1)} %p_hbm.1, f32[1,128]{1,0:T(1,128)} %bitcast.7, f32[1,2048]{1,0:T(1,128)} %bitcast.5, bf16[128,2048]{1,0:T(8,128)(2,1)} %g_hbm.1), custom_call_target="tpu_custom_call" | custom-call | tf_op jit(solution)/shard_map/pallas_call | solution.py:387
  50.6 1.3 %copy.9 = f32[128,8]{0,1:T(8,128)} copy(f32[128,8]{0,1:T(8,128)} %bitcast.6) | data formatting | bytes 8192
  51.9 1.7 %copy.10 = bf16[2048,64]{0,1:T(8,128)(2,1)} copy(bf16[2048,64]{0,1:T(8,128)(2,1)} %bitcast.4) | data formatting | bytes 524288

commit v5 on v4

--- a/solution.py
+++ b/solution.py
@@ -40,6 +40,7 @@
     [(dz, dy) for dz in range(N_Z) for dy in range(N_Y) if dz or dy], key=lambda o: -hops(*o)
 )
 DP_FAR_FIRST = (4, 5, 3, 2, 6, 1, 7)
+FAR = (4, 3, 5, 2, 6, 1, 7)
 
 
 def wait_bytes(ref, sem):
@@ -89,15 +90,16 @@
         load.start()
 
     barrier = pltpu.get_barrier_semaphore()
-    for k in range(1, 8):
+    for k in FAR:
+        pl.semaphore_signal(
+            barrier, inc=1, device_id=(dp, z * N_Y + lax.rem(y + k, N_Y)), device_id_type=MESH
+        )
+        pl.semaphore_signal(
+            barrier, inc=1, device_id=(dp, lax.rem(z + k, N_Z) * N_Y + y), device_id_type=MESH
+        )
+    for k in DP_FAR_FIRST:
         pl.semaphore_signal(
             barrier, inc=1, device_id=(lax.rem(dp + k, N_DP), pr), device_id_type=MESH
-        )
-        pl.semaphore_signal(
-            barrier, inc=1, device_id=(dp, z * N_Y + lax.rem(y + k, N_Y)), device_id_type=MESH
-        )
-        pl.semaphore_signal(
-            barrier, inc=1, device_id=(dp, lax.rem(z + k, N_Z) * N_Y + y), device_id_type=MESH
         )
     for load in loads:
         load.wait()
@@ -141,7 +143,7 @@
 
     pl.semaphore_wait(barrier, 21)
     to_dp(td1, 0)
-    for k in range(1, 8):
+    for k in FAR:
         pl.semaphore_signal(
             ready, inc=1, device_id=(dp, lax.rem(z + k, N_Z) * N_Y + y), device_id_type=MESH
         )
@@ -261,13 +263,6 @@
     wait_bytes(sp_in, recv.at[8])
     for j in range(4):
         sp_own[j] = (sp_own[j].astype(F32) + sp_in[j].astype(F32)).astype(BF16)
-    right, left, across = (lax.rem(x + k, 4) for k in (1, 3, 2))
-    for i, to in enumerate((right, left)):
-        pltpu.make_async_remote_copy(
-            src_ref=sp_own.at[across, pl.ds(32 * i, 32)], dst_ref=s2.at[i],
-            send_sem=send.at[9], recv_sem=recv.at[9],
-            device_id=(2 * to + core, pr), device_id_type=MESH,
-        ).start()
     wait_bytes(td2.at[pl.ds(0, N_DP - 1)], recv.at[2])
     two = jnp.sum(td2[...], axis=0)
     m0 = s0 + total(two[0:1, cols : cols + LANES])
@@ -290,12 +285,11 @@
         axis=0,
     )
     to_proto(lambda other: (tp2.at[pr], tp2.at[pr]), 3)
-    wait_bytes(s2, recv.at[9])
+    right, left, across = (lax.rem(x + k, 4) for k in (1, 3, 2))
     for i, to in enumerate((right, left)):
-        half = pl.ds(32 * i, 32)
-        sp_own[to, half] = (sp_own[to, half].astype(F32) + s2[i].astype(F32)).astype(BF16)
         pltpu.make_async_remote_copy(
-            src_ref=sp_own.at[to], dst_ref=sx.at[i], send_sem=send.at[10], recv_sem=recv.at[10],
+            src_ref=sp_own.at[across, pl.ds(32 * i, 32)], dst_ref=s2.at[i],
+            send_sem=send.at[9], recv_sem=recv.at[9],
             device_id=(2 * to + core, pr), device_id_type=MESH,
         ).start()
     wait_bytes(ef.at[pl.ds(0, 4 * LANES)], recv.at[7])
@@ -318,6 +312,14 @@
         axis=0,
     )
     to_dp(td3, 4)
+    wait_bytes(s2, recv.at[9])
+    for i, to in enumerate((right, left)):
+        half = pl.ds(32 * i, 32)
+        sp_own[to, half] = (sp_own[to, half].astype(F32) + s2[i].astype(F32)).astype(BF16)
+        pltpu.make_async_remote_copy(
+            src_ref=sp_own.at[to], dst_ref=sx.at[i], send_sem=send.at[10], recv_sem=recv.at[10],
+            device_id=(2 * to + core, pr), device_id_type=MESH,
+        ).start()
     five = [
         total(jnp.where((lane >= 32 * g) & (lane < 32 * g + 32), three[r : r + 1], 0.0))
         for r, g in ((2, 0), (2, 1), (2, 2), (2, 3), (3, 0), (3, 1))

time: 53.8 us -> 53.5 us (level)
  no operation moved by 1% of the time
where the time goes in v5:
time: 53.5 us; the launch traced here: 53.3 us
  Pallas kernels  49.7 us (93%)
  local copies, waits for them, and re-layouts  2.95 us (6%)
  between operations  0.64 us (1%)
    pallas_call x1, Pallas kernels, shards(): pl.pallas_call(functools.partial(body, rows * N_DP, cols * N_PROTO), out_...  49.7 us
    unnamed x2, local copies, waits for them, and re-layouts  2.95 us

profile of v5, /device:TPU:1, one launch (start us, length us, event | category | flops | bytes accessed | tf_op | source)
XLA Modules:
  0.0 53.3 jit_solution(1275287896388076034)
XLA Ops:
  0.6 49.7 %shard_map.68 = (f32[8,128]{1,0:T(8,128)}, bf16[64,2048]{1,0:T(8,128)(2,1)}) custom-call(bf16[128,512]{1,0:T(8,128)(2,1)} %e_hbm.1, bf16[2048,512]{1,0:T(8,128)(2,1)} %p_hbm.1, f32[1,128]{1,0:T(1,128)} %bitcast.7, f32[1,2048]{1,0:T(1,128)} %bitcast.5, bf16[128,2048]{1,0:T(8,128)(2,1)} %g_hbm.1), custom_call_target="tpu_custom_call" | custom-call | tf_op jit(solution)/shard_map/pallas_call | solution.py:389
  50.3 1.3 %copy.9 = f32[128,8]{0,1:T(8,128)} copy(f32[128,8]{0,1:T(8,128)} %bitcast.6) | data formatting | bytes 8192
  51.6 1.7 %copy.10 = bf16[2048,64]{0,1:T(8,128)(2,1)} copy(bf16[2048,64]{0,1:T(8,128)(2,1)} %bitcast.4) | data formatting | bytes 524288

commit v6 on v5

--- a/solution.py
+++ b/solution.py
@@ -70,7 +70,7 @@
     e_hbm, p_hbm, er_hbm, pc_hbm, g_hbm, o_emb, o_proto,
     ev, et, pv, er, pc, gv, kv, wv, td1, td2, td3, tp1, tp2, rs_out, rs_in,
     ef, eg, erc, kf, uf, sf, sp_out, sp_own, sp_in, s2, sx,
-    in_sem, ready, send, recv,
+    op, hs, in_sem, send, recv,
 ):
     dp, pr = lax.axis_index("dp"), lax.axis_index("proto")
     z, y = lax.div(pr, N_Y), lax.rem(pr, N_Y)
@@ -120,6 +120,7 @@
                 device_id=(dp, other), device_id_type=MESH,
             ).start()
 
+    hs[z] = jnp.zeros((8, LANES), F32)
     er_col = as_column(er[...])
     row_acc = jnp.zeros((LANES, LANES), F32)
     rhs_acc = jnp.zeros((LANES, LANES), F32)
@@ -144,9 +145,10 @@
     pl.semaphore_wait(barrier, 21)
     to_dp(td1, 0)
     for k in FAR:
-        pl.semaphore_signal(
-            ready, inc=1, device_id=(dp, lax.rem(z + k, N_Z) * N_Y + y), device_id_type=MESH
-        )
+        pltpu.make_async_remote_copy(
+            src_ref=hs.at[z], dst_ref=hs.at[z], send_sem=send.at[11], recv_sem=recv.at[11],
+            device_id=(dp, lax.rem(z + k, N_Z) * N_Y + y), device_id_type=MESH,
+        ).start()
     row_part = as_row(row_acc)
     rhs_part = as_row(rhs_acc)
 
@@ -187,7 +189,7 @@
          jnp.where(lane < 64, by_two(fold(v0c * v0c)), by_two(fold(v0c * dc * v0c)))],
         axis=0,
     )
-    pl.semaphore_wait(ready, 7)
+    wait_bytes(hs.at[pl.ds(0, N_Z - 1)], recv.at[11])
     to_proto(lambda other: (tp1.at[pr], tp1.at[pr]), 1)
 
     x, core = lax.div(dp, 2), lax.rem(dp, 2)
@@ -361,10 +363,14 @@
         at = pl.ds(c * 512, 512)
         terms = jnp.dot(lhs, kf[:, at], preferred_element_type=F32)
         part = sf[:, at] - terms - uf[:, at] * (sol_c - guess)[:, c * 512 : (c + 1) * 512]
-        o_proto[:, at] = (part * (1.0 / TEMP)).astype(BF16)
+        op[:, at] = (part * (1.0 / TEMP)).astype(BF16)
+    store = pltpu.make_async_copy(op, o_proto, in_sem.at[5])
+    store.start()
     wait_bytes(rs_in.at[pl.ds(0, N_PROTO - 1)], recv.at[5])
     o_emb[...] = jnp.sum(rs_in[...].astype(F32), axis=0)
 
+    store.wait()
+    wait_bytes(hs.at[pl.ds(0, N_Z - 1)], send.at[11])
     wait_bytes(td1.at[pl.ds(0, N_DP - 1)], send.at[0])
     wait_bytes(tp1.at[pl.ds(0, N_PROTO - 1)], send.at[1])
     wait_bytes(td2.at[pl.ds(0, N_DP - 1)], send.at[2])
@@ -393,7 +399,7 @@
             jax.ShapeDtypeStruct((share, cols), BF16),
         ),
         in_specs=[any_space] * 5,
-        out_specs=(vmem, vmem),
+        out_specs=(vmem, any_space),
         scratch_shapes=[
             pltpu.VMEM((rows, width), BF16),
             pltpu.VMEM((N_DP, share, rows), BF16),
@@ -421,10 +427,11 @@
             pltpu.VMEM((4, share, cols), BF16),
             pltpu.VMEM((2, share // 2, cols), BF16),
             pltpu.VMEM((2, share, cols), BF16),
-            pltpu.SemaphoreType.DMA((5,)),
-            pltpu.SemaphoreType.REGULAR,
-            pltpu.SemaphoreType.DMA((11,)),
-            pltpu.SemaphoreType.DMA((11,)),
+            pltpu.VMEM((share, cols), BF16),
+            pltpu.VMEM((N_Z, 8, LANES), F32),
+            pltpu.SemaphoreType.DMA((6,)),
+            pltpu.SemaphoreType.DMA((12,)),
+            pltpu.SemaphoreType.DMA((12,)),
         ],
         compiler_params=pltpu.CompilerParams(
             collective_id=0, has_side_effects=True, vmem_limit_bytes=56 * 1024 * 1024

time: 53.5 us -> 54 us (level)
  no operation moved by 1% of the time
where the time goes in v6:
time: 54 us; the launch traced here: 53.7 us
  Pallas kernels  50.2 us (93%)
  local copies, waits for them, and re-layouts  2.95 us (5%)
  between operations  0.64 us (1%)
    pallas_call x1, Pallas kernels, shards(): pl.pallas_call(functools.partial(body, rows * N_DP, cols * N_PROTO), out_...  50.2 us
    unnamed x2, local copies, waits for them, and re-layouts  2.95 us

profile of v6, /device:TPU:1, one launch (start us, length us, event | category | flops | bytes accessed | tf_op | source)
XLA Modules:
  0.0 53.7 jit_solution(6931097787982536353)
XLA Ops:
  0.6 50.2 %shard_map.68 = (f32[8,128]{1,0:T(8,128)}, bf16[64,2048]{1,0:T(8,128)(2,1)}) custom-call(bf16[128,512]{1,0:T(8,128)(2,1)} %e_hbm.1, bf16[2048,512]{1,0:T(8,128)(2,1)} %p_hbm.1, f32[1,128]{1,0:T(1,128)} %bitcast.7, f32[1,2048]{1,0:T(1,128)} %bitcast.5, bf16[128,2048]{1,0:T(8,128)(2,1)} %g_hbm.1), custom_call_target="tpu_custom_call" | custom-call | tf_op jit(solution)/shard_map/pallas_call | solution.py:395
  50.8 1.3 %copy.9 = f32[128,8]{0,1:T(8,128)} copy(f32[128,8]{0,1:T(8,128)} %bitcast.6) | data formatting | bytes 8192
  52.1 1.7 %copy.10 = bf16[2048,64]{0,1:T(8,128)(2,1)} copy(bf16[2048,64]{0,1:T(8,128)(2,1)} %bitcast.4) | data formatting | bytes 524288

commit v7 on v6

--- a/solution.py
+++ b/solution.py
@@ -212,8 +212,9 @@
 
     def weighted_terms(to, first):
         lhs = jnp.concatenate([et[2 * j + first] for j in range(4)], axis=0)
-        for c in range(cols // 512):
-            at = pl.ds(c * 512, 512)
+        @pl.loop(0, cols // 512)
+        def _(c):
+            at = pl.ds(pl.multiple_of(c * 512, 512), 512)
             part = jnp.dot(lhs, wv[:, at], preferred_element_type=F32).astype(BF16)
             for j in range(4):
                 to[j, :, at] = part[64 * j : 64 * j + 64]
@@ -248,7 +249,7 @@
     to_dp(td2, 2)
 
     def whole_kernel(c):
-        at = pl.ds(c * wide, wide)
+        at = pl.ds(pl.multiple_of(c * wide, wide), wide)
         scores = lax.dot_general(
             ef[...], pv[at, :], (((1,), (1,)), ((), ())), preferred_element_type=F32
         )
@@ -297,12 +298,12 @@
     wait_bytes(ef.at[pl.ds(0, 4 * LANES)], recv.at[7])
     for d in range(N_DP):
         eg[d] = ef[d * LANES : (d + 1) * LANES, pl.ds(pl.multiple_of(x * LANES, LANES), LANES)].astype(F32).T
-    for c in range(cols // wide):
-        whole_kernel(c)
+    pl.loop(0, cols // wide)(whole_kernel)
     share = pl.ds(pl.multiple_of(64 * core, 64), 64)
     lhs = jnp.concatenate([eg[d, share, :] for d in range(N_DP)], axis=1).astype(BF16)
-    for c in range(cols // 512):
-        at = pl.ds(c * 512, 512)
+    @pl.loop(0, cols // 512)
+    def _(c):
+        at = pl.ds(pl.multiple_of(c * 512, 512), 512)
         uf[:, at] = jnp.dot(lhs, kf[:, at], preferred_element_type=F32)
     wait_bytes(tp2.at[pl.ds(0, N_PROTO - 1)], recv.at[3])
     three = jnp.sum(tp2[...], axis=0)

time: 54 us -> 53.8 us (level)
  no operation moved by 1% of the time
where the time goes in v7:
time: 53.8 us; the launch traced here: 53.6 us
  Pallas kernels  50 us (93%)
  local copies, waits for them, and re-layouts  2.95 us (5%)
  between operations  0.64 us (1%)
    pallas_call x1, Pallas kernels, shards(): pl.pallas_call(functools.partial(body, rows * N_DP, cols * N_PROTO), out_...  50 us
    unnamed x2, local copies, waits for them, and re-layouts  2.95 us

profile of v7, /device:TPU:1, one launch (start us, length us, event | category | flops | bytes accessed | tf_op | source)
XLA Modules:
  0.0 53.6 jit_solution(12122609329094296815)
XLA Ops:
  0.6 50.0 %shard_map.68 = (f32[8,128]{1,0:T(8,128)}, bf16[64,2048]{1,0:T(8,128)(2,1)}) custom-call(bf16[128,512]{1,0:T(8,128)(2,1)} %e_hbm.1, bf16[2048,512]{1,0:T(8,128)(2,1)} %p_hbm.1, f32[1,128]{1,0:T(1,128)} %bitcast.7, f32[1,2048]{1,0:T(1,128)} %bitcast.5, bf16[128,2048]{1,0:T(8,128)(2,1)} %g_hbm.1), custom_call_target="tpu_custom_call" | custom-call | tf_op jit(solution)/shard_map/pallas_call | solution.py:396
  50.6 1.3 %copy.9 = f32[128,8]{0,1:T(8,128)} copy(f32[128,8]{0,1:T(8,128)} %bitcast.6) | data formatting | bytes 8192
  51.9 1.7 %copy.10 = bf16[2048,64]{0,1:T(8,128)(2,1)} copy(bf16[2048,64]{0,1:T(8,128)(2,1)} %bitcast.4) | data formatting | bytes 524288

commit v8 on v5

--- a/solution.py
+++ b/solution.py
@@ -70,7 +70,7 @@
     e_hbm, p_hbm, er_hbm, pc_hbm, g_hbm, o_emb, o_proto,
     ev, et, pv, er, pc, gv, kv, wv, td1, td2, td3, tp1, tp2, rs_out, rs_in,
     ef, eg, erc, kf, uf, sf, sp_out, sp_own, sp_in, s2, sx,
-    in_sem, ready, send, recv,
+    op, in_sem, ready, send, recv,
 ):
     dp, pr = lax.axis_index("dp"), lax.axis_index("proto")
     z, y = lax.div(pr, N_Y), lax.rem(pr, N_Y)
@@ -361,10 +361,13 @@
         at = pl.ds(c * 512, 512)
         terms = jnp.dot(lhs, kf[:, at], preferred_element_type=F32)
         part = sf[:, at] - terms - uf[:, at] * (sol_c - guess)[:, c * 512 : (c + 1) * 512]
-        o_proto[:, at] = (part * (1.0 / TEMP)).astype(BF16)
+        op[:, at] = (part * (1.0 / TEMP)).astype(BF16)
+    store = pltpu.make_async_copy(op, o_proto, in_sem.at[5])
+    store.start()
     wait_bytes(rs_in.at[pl.ds(0, N_PROTO - 1)], recv.at[5])
     o_emb[...] = jnp.sum(rs_in[...].astype(F32), axis=0)
 
+    store.wait()
     wait_bytes(td1.at[pl.ds(0, N_DP - 1)], send.at[0])
     wait_bytes(tp1.at[pl.ds(0, N_PROTO - 1)], send.at[1])
     wait_bytes(td2.at[pl.ds(0, N_DP - 1)], send.at[2])
@@ -393,7 +396,7 @@
             jax.ShapeDtypeStruct((share, cols), BF16),
         ),
         in_specs=[any_space] * 5,
-        out_specs=(vmem, vmem),
+        out_specs=(vmem, any_space),
         scratch_shapes=[
             pltpu.VMEM((rows, width), BF16),
             pltpu.VMEM((N_DP, share, rows), BF16),
@@ -421,7 +424,8 @@
             pltpu.VMEM((4, share, cols), BF16),
             pltpu.VMEM((2, share // 2, cols), BF16),
             pltpu.VMEM((2, share, cols), BF16),
-            pltpu.SemaphoreType.DMA((5,)),
+            pltpu.VMEM((share, cols), BF16),
+            pltpu.SemaphoreType.DMA((6,)),
             pltpu.SemaphoreType.REGULAR,
             pltpu.SemaphoreType.DMA((11,)),
             pltpu.SemaphoreType.DMA((11,)),

time: 53.5 us -> 53.4 us (level)
  no operation moved by 1% of the time
where the time goes in v8:
time: 53.4 us; the launch traced here: 53.2 us
  Pallas kernels  49.6 us (93%)
  local copies, waits for them, and re-layouts  2.95 us (6%)
  between operations  0.64 us (1%)
    pallas_call x1, Pallas kernels, shards(): pl.pallas_call(functools.partial(body, rows * N_DP, cols * N_PROTO), out_...  49.6 us
    unnamed x2, local copies, waits for them, and re-layouts  2.95 us

profile of v8, /device:TPU:1, one launch (start us, length us, event | category | flops | bytes accessed | tf_op | source)
XLA Modules:
  0.0 53.2 jit_solution(1302743427210107953)
XLA Ops:
  0.6 49.6 %shard_map.68 = (f32[8,128]{1,0:T(8,128)}, bf16[64,2048]{1,0:T(8,128)(2,1)}) custom-call(bf16[128,512]{1,0:T(8,128)(2,1)} %e_hbm.1, bf16[2048,512]{1,0:T(8,128)(2,1)} %p_hbm.1, f32[1,128]{1,0:T(1,128)} %bitcast.7, f32[1,2048]{1,0:T(1,128)} %bitcast.5, bf16[128,2048]{1,0:T(8,128)(2,1)} %g_hbm.1), custom_call_target="tpu_custom_call" | custom-call | tf_op jit(solution)/shard_map/pallas_call | solution.py:392
  50.3 1.3 %copy.9 = f32[128,8]{0,1:T(8,128)} copy(f32[128,8]{0,1:T(8,128)} %bitcast.6) | data formatting | bytes 8192
  51.5 1.7 %copy.10 = bf16[2048,64]{0,1:T(8,128)(2,1)} copy(bf16[2048,64]{0,1:T(8,128)(2,1)} %bitcast.4) | data formatting | bytes 524288
